TPU v7x, 32 devices: a whole 2x2x4 slice. The times are simulated.
32 devices in a mesh: tx: 8 (over y, x, core), ty: 4 (over z).
Axes of the slice: x: 2, y: 2, z: 4, core: 2. Of those that a mesh axis runs over, the one named last changes fastest.
Arguments:
- volume: bfloat16 [256, 128, 16, 64], P('tx', 'ty'), may hold values from -6 to 6
- first_weight: bfloat16 [2, 2, 2, 64, 128], replicated, may hold values from -0.375 to 0.375
- first_bias: float32 [128], replicated, may hold values from -1.5 to 1.5
- second_weight: bfloat16 [2, 2, 2, 128, 256], replicated, may hold values from -0.25 to 0.25
- second_bias: float32 [256], replicated, may hold values from -1.5 to 1.5
- inner_weight: bfloat16 [3, 3, 3, 256, 256], replicated, may hold values from -0.109375 to 0.109375
- inner_bias: float32 [256], replicated, may hold values from -1.5 to 1.5
- outer_weight: bfloat16 [3, 3, 3, 256, 256], replicated, may hold values from -0.109375 to 0.109375
- outer_bias: float32 [256], replicated, may hold values from -1.5 to 1.5
Outputs:
- encoded: bfloat16 [64, 32, 4, 256], P('tx', 'ty')
All inputs are finite; a program needn't handle non-finite values.
Results may differ from a plain program's by a relative error of at most 0.0058.
Values may be sent and summed in bfloat16 or wider, within the bound.
A program may use at most 64 MiB of HBM per device.

v0:
```python
import jax
import jax.numpy as jnp
from jax import lax
from jax.sharding import PartitionSpec as P

DILATION_RATE = 2


def extended(shard, sides, width):
    for axis, dim in sides:
        count, length = (lax.axis_size(axis), shard.shape[dim])
        up = [(i, (i + 1) % count) for i in range(count - 1)]
        down = [(j, i) for i, j in up]
        last = lax.slice_in_dim(shard, length - width, length, axis=dim)
        initial = lax.slice_in_dim(shard, 0, width, axis=dim)
        before = lax.ppermute(last, axis, up)
        after = lax.ppermute(initial, axis, down)
        shard = jnp.concatenate([before, shard, after], axis=dim)
    return shard


def leaky(values):
    return jnp.where(values > 0, values, 0.01 * values)


def strided(feature_field, weight, bias):
    size_x, size_y, size_z, chans = feature_field.shape
    blocks = feature_field.reshape(size_x // 2, 2, size_y // 2, 2, size_z // 2, 2, chans)
    blocks = blocks.transpose(0, 2, 4, 1, 3, 5, 6).reshape(-1, 8 * chans)
    total = jnp.dot(blocks, weight.reshape(8 * chans, -1), preferred_element_type=jnp.float32)
    return (
        leaky(total + bias).astype(jnp.bfloat16).reshape(size_x // 2, size_y // 2, size_z // 2, -1)
    )


def dilated_sum(padded_volume, weight):
    output_x = padded_volume.shape[0] - 2 * DILATION_RATE
    output_y = padded_volume.shape[1] - 2 * DILATION_RATE
    output_z = padded_volume.shape[2] - 2 * DILATION_RATE
    chans = padded_volume.shape[3]
    total = jnp.zeros((output_x * output_y * output_z, weight.shape[4]), jnp.float32)
    for shift_along_x in range(3):
        for shift_along_y in range(3):
            for shift_along_z in range(3):
                volume_portion = padded_volume[
                    shift_along_x * DILATION_RATE : shift_along_x * DILATION_RATE + output_x,
                    shift_along_y * DILATION_RATE : shift_along_y * DILATION_RATE + output_y,
                    shift_along_z * DILATION_RATE : shift_along_z * DILATION_RATE + output_z,
                    :,
                ]
                total = total + jnp.dot(
                    volume_portion.reshape(-1, chans),
                    weight[shift_along_x, shift_along_y, shift_along_z],
                    preferred_element_type=jnp.float32,
                )
    return total.reshape(output_x, output_y, output_z, -1)


def padding_depth(feature_field):
    return jnp.pad(feature_field, ((0, 0), (0, 0), (DILATION_RATE, DILATION_RATE), (0, 0)))


def local(
    volume,
    first_weight,
    first_bias,
    second_weight,
    second_bias,
    inner_weight,
    inner_bias,
    outer_weight,
    outer_bias,
):
    finer = strided(volume, first_weight, first_bias)
    coarse_volume = strided(finer, second_weight, second_bias)
    padded_volume = padding_depth(extended(coarse_volume, (("tx", 0), ("ty", 1)), DILATION_RATE))
    hidden_activation = leaky(dilated_sum(padded_volume, inner_weight) + inner_bias).astype(
        jnp.bfloat16
    )
    padded_volume = padding_depth(
        extended(hidden_activation, (("tx", 0), ("ty", 1)), DILATION_RATE)
    )
    result = leaky(
        coarse_volume.astype(jnp.float32) + dilated_sum(padded_volume, outer_weight) + outer_bias
    )
    return result.astype(jnp.bfloat16)


def solution(mesh):
    in_specs = (P("tx", "ty", None, None), P(), P(), P(), P(), P(), P(), P(), P())
    out_specs = P("tx", "ty", None, None)
    return jax.shard_map(local, mesh=mesh, in_specs=in_specs, out_specs=out_specs, check_vma=False)
```

profile of v0, /device:TPU:11, one launch (start us, length us, event | category | flops | bytes accessed | tf_op | source)
XLA Modules:
  0.0 121.8 jit_solution(14016037181336260660)
XLA Ops:
  0.0 8.8 %copy.14 = bf16[16,2,16,2,8,2,64]{6,5,3,1,4,2,0:T(2,128)(2,1)} copy(bf16[16,2,16,2,8,2,64]{6,5,4,3,2,1,0:T(2,128)(2,1)} %bitcast.231) | data formatting | bytes 4194304 | tf_op jit(solution)/shard_map/reshape | solution.py:28
  8.8 9.4 %reshape.190 = bf16[2048,512]{1,0:T(8,128)(2,1)S(1)} reshape(bf16[16,16,8,2,2,2,64]{6,5,4,3,2,1,0:T(2,128)(2,1)} %bitcast.230) | data formatting | bytes 4194304 | tf_op jit(solution)/shard_map/reshape | solution.py:29
  20.0 3.7 %collective-permute-start = (bf16[2,8,4,256]{3,2,1,0:T(4,128)(2,1)S(1)}, bf16[2,8,4,256]{3,2,1,0:T(4,128)(2,1)S(1)}, u32[]{:S(2)}, u32[]{:S(2)}) collective-permute-start(bf16[2,8,4,256]{3,2,1,0:T(4,128)(2,1)S(1)} %slice.391), channel_id=1, source_target_pairs={{0,4},{4,8},{8,12},{12,16},{16,20},{20,24},{24,28},{1,5},{5,9},{9,... | collective-permute-start | bytes 98312 | tf_op jit(solution)/shard_map/ppermute | solution.py:16
  23.7 1.9 %collective-permute-start.1 = (bf16[2,8,4,256]{3,2,1,0:T(4,128)(2,1)S(1)}, bf16[2,8,4,256]{3,2,1,0:T(4,128)(2,1)S(1)}, u32[]{:S(2)}, u32[]{:S(2)}) collective-permute-start(bf16[2,8,4,256]{3,2,1,0:T(4,128)(2,1)S(1)} %slice.393), channel_id=1, source_target_pairs={{4,0},{8,4},{12,8},{16,12},{20,16},{24,20},{28,24},{5,1},{9,5},{13... | collective-permute-start | bytes 98312 | tf_op jit(solution)/shard_map/ppermute | solution.py:17
  25.7 4.1 %collective-permute-done.1 = bf16[2,8,4,256]{3,2,1,0:T(4,128)(2,1)S(1)} collective-permute-done((bf16[2,8,4,256]{3,2,1,0:T(4,128)(2,1)S(1)}, bf16[2,8,4,256]{3,2,1,0:T(4,128)(2,1)S(1)}, u32[]{:S(2)}, u32[]{:S(2)}) %collective-permute-start.1) | collective-permute-done | bytes 32800 | tf_op jit(solution)/shard_map/ppermute | solution.py:17
  30.2 3.2 %collective-permute-start.2 = (bf16[12,2,4,256]{3,2,1,0:T(4,128)(2,1)S(1)}, bf16[12,2,4,256]{3,2,1,0:T(4,128)(2,1)S(1)}, u32[]{:S(2)}, u32[]{:S(2)}) collective-permute-start(bf16[12,2,4,256]{3,2,1,0:T(4,128)(2,1)S(1)} %get-tuple-element.60), channel_id=1, source_target_pairs={{0,1},{1,2},{2,3},{4,5},{5,6},{6,7},{8,9},{9,10},{10,11},{12,13},{... | collective-permute-start | bytes 147464 | tf_op jit(solution)/shard_map/ppermute | solution.py:16
  33.4 2.3 %collective-permute-start.3 = (bf16[12,2,4,256]{3,2,1,0:T(4,128)(2,1)S(1)}, bf16[12,2,4,256]{3,2,1,0:T(4,128)(2,1)S(1)}, u32[]{:S(2)}, u32[]{:S(2)}) collective-permute-start(bf16[12,2,4,256]{3,2,1,0:T(4,128)(2,1)S(1)} %get-tuple-element.61), channel_id=1, source_target_pairs={{1,0},{2,1},{3,2},{5,4},{6,5},{7,6},{9,8},{10,9},{11,10},{13,12},{... | collective-permute-start | bytes 147464 | tf_op jit(solution)/shard_map/ppermute | solution.py:17
  37.0 1.2 collective-permute-done.3
  42.4 1.2 fusion.149
  45.5 1.1 fusion.65
  49.7 1.1 fusion.81
  52.2 1.1 fusion.87
  53.3 1.1 convolution_add_fusion.46
  54.4 1.2 convolution_add_fusion.45
  55.6 1.2 convolution_add_fusion.44
  56.8 1.2 fusion.7
  57.9 1.1 convolution_add_fusion.42
  59.0 1.1 convolution_add_fusion.41
  60.2 1.1 convolution_add_fusion.40
  61.3 1.1 convolution_add_fusion.39
  62.4 1.1 convolution_add_fusion.38
  63.6 1.1 convolution_add_fusion.37
  64.7 1.1 convolution_add_fusion.36
  65.8 1.1 convolution_add_fusion.35
  68.1 1.1 convolution_add_fusion.34
  69.2 1.1 convolution_add_fusion.33
  70.3 1.1 convolution_add_fusion.32
  71.4 1.1 convolution_add_fusion.31
  72.6 1.1 convolution_add_fusion.30
  73.7 1.1 fusion.6
  74.8 1.1 convolution_add_fusion.28
  75.9 1.1 fusion.5
  77.0 1.1 convolution_add_fusion.26
  78.1 1.1 fusion.4
  79.4 3.3 %collective-permute-start.4 = (bf16[2,8,4,256]{3,2,1,0:T(4,128)(2,1)S(1)}, bf16[2,8,4,256]{3,2,1,0:T(4,128)(2,1)S(1)}, u32[]{:S(2)}, u32[]{:S(2)}) collective-permute-start(bf16[2,8,4,256]{3,2,1,0:T(4,128)(2,1)S(1)} %get-tuple-element.64), channel_id=1, source_target_pairs={{0,4},{4,8},{8,12},{12,16},{16,20},{20,24},{24,28},{1,5},{5,9},{9,... | collective-permute-start | bytes 98312 | tf_op jit(solution)/shard_map/ppermute | solution.py:16
  82.8 1.9 %collective-permute-start.5 = (bf16[2,8,4,256]{3,2,1,0:T(4,128)(2,1)S(1)}, bf16[2,8,4,256]{3,2,1,0:T(4,128)(2,1)S(1)}, u32[]{:S(2)}, u32[]{:S(2)}) collective-permute-start(bf16[2,8,4,256]{3,2,1,0:T(4,128)(2,1)S(1)} %get-tuple-element.65), channel_id=1, source_target_pairs={{4,0},{8,4},{12,8},{16,12},{20,16},{24,20},{28,24},{5,1},{9,5},{13... | collective-permute-start | bytes 98312 | tf_op jit(solution)/shard_map/ppermute | solution.py:17
  84.7 4.2 %collective-permute-done.5 = bf16[2,8,4,256]{3,2,1,0:T(4,128)(2,1)S(1)} collective-permute-done((bf16[2,8,4,256]{3,2,1,0:T(4,128)(2,1)S(1)}, bf16[2,8,4,256]{3,2,1,0:T(4,128)(2,1)S(1)}, u32[]{:S(2)}, u32[]{:S(2)}) %collective-permute-start.5) | collective-permute-done | bytes 32800 | tf_op jit(solution)/shard_map/ppermute | solution.py:17
  89.0 3.2 %collective-permute-start.6 = (bf16[12,2,4,256]{3,2,1,0:T(4,128)(2,1)S(1)}, bf16[12,2,4,256]{3,2,1,0:T(4,128)(2,1)S(1)}, u32[]{:S(2)}, u32[]{:S(2)}) collective-permute-start(bf16[12,2,4,256]{3,2,1,0:T(4,128)(2,1)S(1)} %get-tuple-element.55), channel_id=1, source_target_pairs={{0,1},{1,2},{2,3},{4,5},{5,6},{6,7},{8,9},{9,10},{10,11},{12,13},{... | collective-permute-start | bytes 147464 | tf_op jit(solution)/shard_map/ppermute | solution.py:16
  92.2 2.1 %collective-permute-start.7 = (bf16[12,2,4,256]{3,2,1,0:T(4,128)(2,1)S(1)}, bf16[12,2,4,256]{3,2,1,0:T(4,128)(2,1)S(1)}, u32[]{:S(2)}, u32[]{:S(2)}) collective-permute-start(bf16[12,2,4,256]{3,2,1,0:T(4,128)(2,1)S(1)} %get-tuple-element.56), channel_id=1, source_target_pairs={{1,0},{2,1},{3,2},{5,4},{6,5},{7,6},{9,8},{10,9},{11,10},{13,12},{... | collective-permute-start | bytes 147464 | tf_op jit(solution)/shard_map/ppermute | solution.py:17
  95.9 1.2 collective-permute-done.7
  100.8 1.2 fusion.148
  106.5 1.1 fusion.30
  107.7 1.1 fusion.49
  110.9 1.3 %fusion.55 = f32[256,256]{1,0:T(8,128)S(1)} fusion(bf16[256,256]{1,0:T(8,128)(2,1)} %reshape.222, bf16[3,3,3,256,256]{4,3,2,1,0:T(8,128)(2,1)} %param.16), kind=kOutput, calls=%fused_computation.129 | convolution fusion | flops 33554432 | bytes 524288 | tf_op jit(solution)/shard_map/dot_general | solution.py:51
  112.3 1.1 convolution_add_fusion.24
  113.4 1.2 convolution_add_fusion.23
  114.5 1.2 convolution_add_fusion.22
  115.7 1.2 fusion.3
  (154 shorter events, 31.9 us)
Async XLA Ops:
  0.0 19.7 %copy-start = (bf16[2,2,2,128,256]{4,3,2,1,0:T(8,128)(2,1)S(1)}, bf16[2,2,2,128,256]{4,3,2,1,0:T(8,128)(2,1)}, u32[]{:S(2)}) copy-start(bf16[2,2,2,128,256]{4,3,2,1,0:T(8,128)(2,1)} %param.12) | copy-start | bytes 1572868
  8.8 9.4 %copy-start.23 = (bf16[2,2,2,64,128]{4,3,2,1,0:T(8,128)(2,1)S(1)}, bf16[2,2,2,64,128]{4,3,2,1,0:T(8,128)(2,1)}, u32[]{:S(2)}) copy-start(bf16[2,2,2,64,128]{4,3,2,1,0:T(8,128)(2,1)} %param.10) | copy-start | bytes 393220
  8.8 9.4 %copy-start.25 = (f32[128]{0:T(128)S(1)}, f32[128]{0:T(128)}, u32[]{:S(2)}) copy-start(f32[128]{0:T(128)} %param.11) | copy-start | bytes 1540
  18.2 1.5 %copy-start.24 = (f32[256]{0:T(256)S(1)}, f32[256]{0:T(256)}, u32[]{:S(2)}) copy-start(f32[256]{0:T(256)} %param.13) | copy-start | bytes 3076
  20.0 5.7 %collective-permute-start = (bf16[2,8,4,256]{3,2,1,0:T(4,128)(2,1)S(1)}, bf16[2,8,4,256]{3,2,1,0:T(4,128)(2,1)S(1)}, u32[]{:S(2)}, u32[]{:S(2)}) collective-permute-start(bf16[2,8,4,256]{3,2,1,0:T(4,128)(2,1)S(1)} %slice.391), channel_id=1, source_target_pairs={{0,4},{4,8},{8,12},{12,16},{16,20},{20,24},{24,28},{1,5},{5,9},{9,... | collective-permute-start | bytes 98312 | tf_op jit(solution)/shard_map/ppermute | solution.py:16
  23.7 6.1 %collective-permute-start.1 = (bf16[2,8,4,256]{3,2,1,0:T(4,128)(2,1)S(1)}, bf16[2,8,4,256]{3,2,1,0:T(4,128)(2,1)S(1)}, u32[]{:S(2)}, u32[]{:S(2)}) collective-permute-start(bf16[2,8,4,256]{3,2,1,0:T(4,128)(2,1)S(1)} %slice.393), channel_id=1, source_target_pairs={{4,0},{8,4},{12,8},{16,12},{20,16},{24,20},{28,24},{5,1},{9,5},{13... | collective-permute-start | bytes 98312 | tf_op jit(solution)/shard_map/ppermute | solution.py:17
  30.2 6.9 %collective-permute-start.2 = (bf16[12,2,4,256]{3,2,1,0:T(4,128)(2,1)S(1)}, bf16[12,2,4,256]{3,2,1,0:T(4,128)(2,1)S(1)}, u32[]{:S(2)}, u32[]{:S(2)}) collective-permute-start(bf16[12,2,4,256]{3,2,1,0:T(4,128)(2,1)S(1)} %get-tuple-element.60), channel_id=1, source_target_pairs={{0,1},{1,2},{2,3},{4,5},{5,6},{6,7},{8,9},{9,10},{10,11},{12,13},{... | collective-permute-start | bytes 147464 | tf_op jit(solution)/shard_map/ppermute | solution.py:16
  33.4 4.8 %collective-permute-start.3 = (bf16[12,2,4,256]{3,2,1,0:T(4,128)(2,1)S(1)}, bf16[12,2,4,256]{3,2,1,0:T(4,128)(2,1)S(1)}, u32[]{:S(2)}, u32[]{:S(2)}) collective-permute-start(bf16[12,2,4,256]{3,2,1,0:T(4,128)(2,1)S(1)} %get-tuple-element.61), channel_id=1, source_target_pairs={{1,0},{2,1},{3,2},{5,4},{6,5},{7,6},{9,8},{10,9},{11,10},{13,12},{... | collective-permute-start | bytes 147464 | tf_op jit(solution)/shard_map/ppermute | solution.py:17
  47.4 6.0 %copy-start.10 = (bf16[256,256]{1,0:T(8,128)(2,1)S(1)}, bf16[256,256]{1,0:T(8,128)(2,1)}, u32[]{:S(2)}) copy-start(bf16[256,256]{1,0:T(8,128)(2,1)} %reshape.196) | copy-start | bytes 393220
  48.2 10.8 %copy-start.7 = (bf16[256,256]{1,0:T(8,128)(2,1)S(1)}, bf16[256,256]{1,0:T(8,128)(2,1)}, u32[]{:S(2)}) copy-start(bf16[256,256]{1,0:T(8,128)(2,1)} %reshape.202) | copy-start | bytes 393220
  50.8 10.5 %copy-start.13 = (bf16[256,256]{1,0:T(8,128)(2,1)S(1)}, bf16[256,256]{1,0:T(8,128)(2,1)}, u32[]{:S(2)}) copy-start(bf16[256,256]{1,0:T(8,128)(2,1)} %reshape.204) | copy-start | bytes 393220
  51.5 6.5 %copy-start.16 = (bf16[256,256]{1,0:T(8,128)(2,1)S(1)}, bf16[256,256]{1,0:T(8,128)(2,1)}, u32[]{:S(2)}) copy-start(bf16[256,256]{1,0:T(8,128)(2,1)} %reshape.201) | copy-start | bytes 393220
  52.2 10.2 %copy-start.5 = (bf16[256,256]{1,0:T(8,128)(2,1)S(1)}, bf16[256,256]{1,0:T(8,128)(2,1)}, u32[]{:S(2)}) copy-start(bf16[256,256]{1,0:T(8,128)(2,1)} %reshape.205) | copy-start | bytes 393220
  59.0 10.1 %copy-start.11 = (bf16[256,256]{1,0:T(8,128)(2,1)S(1)}, bf16[256,256]{1,0:T(8,128)(2,1)}, u32[]{:S(2)}) copy-start(bf16[256,256]{1,0:T(8,128)(2,1)} %reshape.209) | copy-start | bytes 393220
  62.4 10.1 %copy-start.8 = (bf16[256,256]{1,0:T(8,128)(2,1)S(1)}, bf16[256,256]{1,0:T(8,128)(2,1)}, u32[]{:S(2)}) copy-start(bf16[256,256]{1,0:T(8,128)(2,1)} %reshape.212) | copy-start | bytes 393220
  63.6 10.1 %copy-start.20 = (bf16[256,256]{1,0:T(8,128)(2,1)S(1)}, bf16[256,256]{1,0:T(8,128)(2,1)}, u32[]{:S(2)}) copy-start(bf16[256,256]{1,0:T(8,128)(2,1)} %reshape.213) | copy-start | bytes 393220
  65.8 10.1 %copy-start.18 = (bf16[256,256]{1,0:T(8,128)(2,1)S(1)}, bf16[256,256]{1,0:T(8,128)(2,1)}, u32[]{:S(2)}) copy-start(bf16[256,256]{1,0:T(8,128)(2,1)} %reshape.216) | copy-start | bytes 393220
  69.2 8.9 %copy-start.19 = (bf16[256,256]{1,0:T(8,128)(2,1)S(1)}, bf16[256,256]{1,0:T(8,128)(2,1)}, u32[]{:S(2)}) copy-start(bf16[256,256]{1,0:T(8,128)(2,1)} %reshape.219) | copy-start | bytes 393220
  71.4 7.9 %copy-start.21 = (f32[256]{0:T(256)S(1)}, f32[256]{0:T(256)}, u32[]{:S(2)}) copy-start(f32[256]{0:T(256)} %param.15) | copy-start | bytes 3076
  79.4 5.3 %collective-permute-start.4 = (bf16[2,8,4,256]{3,2,1,0:T(4,128)(2,1)S(1)}, bf16[2,8,4,256]{3,2,1,0:T(4,128)(2,1)S(1)}, u32[]{:S(2)}, u32[]{:S(2)}) collective-permute-start(bf16[2,8,4,256]{3,2,1,0:T(4,128)(2,1)S(1)} %get-tuple-element.64), channel_id=1, source_target_pairs={{0,4},{4,8},{8,12},{12,16},{16,20},{20,24},{24,28},{1,5},{5,9},{9,... | collective-permute-start | bytes 98312 | tf_op jit(solution)/shard_map/ppermute | solution.py:16
  82.8 6.1 %collective-permute-start.5 = (bf16[2,8,4,256]{3,2,1,0:T(4,128)(2,1)S(1)}, bf16[2,8,4,256]{3,2,1,0:T(4,128)(2,1)S(1)}, u32[]{:S(2)}, u32[]{:S(2)}) collective-permute-start(bf16[2,8,4,256]{3,2,1,0:T(4,128)(2,1)S(1)} %get-tuple-element.65), channel_id=1, source_target_pairs={{4,0},{8,4},{12,8},{16,12},{20,16},{24,20},{28,24},{5,1},{9,5},{13... | collective-permute-start | bytes 98312 | tf_op jit(solution)/shard_map/ppermute | solution.py:17
  89.0 6.9 %collective-permute-start.6 = (bf16[12,2,4,256]{3,2,1,0:T(4,128)(2,1)S(1)}, bf16[12,2,4,256]{3,2,1,0:T(4,128)(2,1)S(1)}, u32[]{:S(2)}, u32[]{:S(2)}) collective-permute-start(bf16[12,2,4,256]{3,2,1,0:T(4,128)(2,1)S(1)} %get-tuple-element.55), channel_id=1, source_target_pairs={{0,1},{1,2},{2,3},{4,5},{5,6},{6,7},{8,9},{9,10},{10,11},{12,13},{... | collective-permute-start | bytes 147464 | tf_op jit(solution)/shard_map/ppermute | solution.py:16
  92.2 4.8 %collective-permute-start.7 = (bf16[12,2,4,256]{3,2,1,0:T(4,128)(2,1)S(1)}, bf16[12,2,4,256]{3,2,1,0:T(4,128)(2,1)S(1)}, u32[]{:S(2)}, u32[]{:S(2)}) collective-permute-start(bf16[12,2,4,256]{3,2,1,0:T(4,128)(2,1)S(1)} %get-tuple-element.56), channel_id=1, source_target_pairs={{1,0},{2,1},{3,2},{5,4},{6,5},{7,6},{9,8},{10,9},{11,10},{13,12},{... | collective-permute-start | bytes 147464 | tf_op jit(solution)/shard_map/ppermute | solution.py:17
  103.6 8.6 %copy-start.9 = (bf16[256,256]{1,0:T(8,128)(2,1)S(1)}, bf16[256,256]{1,0:T(8,128)(2,1)}, u32[]{:S(2)}) copy-start(bf16[256,256]{1,0:T(8,128)(2,1)} %reshape.223) | copy-start | bytes 393220
  105.1 11.9 %copy-start.6 = (bf16[256,256]{1,0:T(8,128)(2,1)S(1)}, bf16[256,256]{1,0:T(8,128)(2,1)}, u32[]{:S(2)}) copy-start(bf16[256,256]{1,0:T(8,128)(2,1)} %reshape.229) | copy-start | bytes 393220
  109.5 7.7 %copy-start.14 = (bf16[256,256]{1,0:T(8,128)(2,1)S(1)}, bf16[256,256]{1,0:T(8,128)(2,1)}, u32[]{:S(2)}) copy-start(bf16[256,256]{1,0:T(8,128)(2,1)} %reshape.230) | copy-start | bytes 393220
  110.9 5.9 %copy-start.1 = (bf16[3,3,3,256,256]{4,3,2,1,0:T(8,128)(2,1)S(1)}, bf16[3,3,3,256,256]{4,3,2,1,0:T(8,128)(2,1)}, u32[]{:S(2)}) copy-start(bf16[3,3,3,256,256]{4,3,2,1,0:T(8,128)(2,1)} %param.16) | copy-start | bytes 10616836
  110.9 5.9 %copy-start.15 = (bf16[256,256]{1,0:T(8,128)(2,1)S(1)}, bf16[256,256]{1,0:T(8,128)(2,1)}, u32[]{:S(2)}) copy-start(bf16[256,256]{1,0:T(8,128)(2,1)} %reshape.228) | copy-start | bytes 393220
  110.9 6.7 %copy-start.4 = (bf16[256,256]{1,0:T(8,128)(2,1)S(1)}, bf16[256,256]{1,0:T(8,128)(2,1)}, u32[]{:S(2)}) copy-start(bf16[256,256]{1,0:T(8,128)(2,1)} %reshape.232) | copy-start | bytes 393220
  116.9 1.8 %copy-start.12 = (bf16[256,256]{1,0:T(8,128)(2,1)S(1)}, bf16[256,256]{1,0:T(8,128)(2,1)}, u32[]{:S(2)}) copy-start(bf16[256,256]{1,0:T(8,128)(2,1)} %reshape.236) | copy-start | bytes 393220
  117.7 1.8 %copy-start.2 = (bf16[256,256]{1,0:T(8,128)(2,1)S(1)}, bf16[256,256]{1,0:T(8,128)(2,1)}, u32[]{:S(2)}) copy-start(bf16[256,256]{1,0:T(8,128)(2,1)} %reshape.240) | copy-start | bytes 393220
  118.3 1.8 %copy-start.17 = (bf16[256,256]{1,0:T(8,128)(2,1)S(1)}, bf16[256,256]{1,0:T(8,128)(2,1)}, u32[]{:S(2)}) copy-start(bf16[256,256]{1,0:T(8,128)(2,1)} %reshape.243) | copy-start | bytes 393220
  118.9 1.8 %copy-start.3 = (bf16[256,256]{1,0:T(8,128)(2,1)S(1)}, bf16[256,256]{1,0:T(8,128)(2,1)}, u32[]{:S(2)}) copy-start(bf16[256,256]{1,0:T(8,128)(2,1)} %reshape.247) | copy-start | bytes 393220
  119.3 1.7 %copy-start.22 = (f32[256]{0:T(256)S(1)}, f32[256]{0:T(256)}, u32[]{:S(2)}) copy-start(f32[256]{0:T(256)} %param.17) | copy-start | bytes 3076
where the time goes:
time: 123 us; the launch traced here: 122 us
  local copies, waits for them, and re-layouts  43 us (35%)
  matrix products  42.9 us (35%)
  starting transfers between devices  21.6 us (18%)
  waiting for transfers between devices  10.7 us (9%)
  other arithmetic  2.55 us (2%)
    dot_general x54, matrix products, dilated_sum(): jnp.dot(volume_portion.reshape(-1, chans), weight[shift_along_x, shift_al...  41.9 us
    reshape x52, local copies, waits for them, and re-layouts, dilated_sum(): volume_portion.reshape(-1, chans)  20.9 us
    ppermute x4, starting transfers between devices, extended(): before = lax.ppermute(last, axis, up)  13.4 us
    ppermute x4, waiting for transfers between devices, extended(): after = lax.ppermute(initial, axis, down)  10.7 us
    reshape x2, local copies, waits for them, and re-layouts, strided(): blocks = blocks.transpose(0, 2, 4, 1, 3, 5, 6).reshape(-1, 8 * chans)  9.75 us
    reshape x1, local copies, waits for them, and re-layouts, strided(): feature_field.reshape(size_x // 2, 2, size_y // 2, 2, size_z // 2, 2, chans)  8.75 us
    ppermute x4, starting transfers between devices, extended(): after = lax.ppermute(initial, axis, down)  8.17 us
    slice x3, local copies, waits for them, and re-layouts, dilated_sum(): padded_volume[shift_along_x * DILATION_RATE:shift_along_x * DILATION_RATE...  2.78 us
  transfers between devices with their start and end apart: 8, of which 4 were waited for; matrix products, arithmetic and copies ran while one was open for 2% of the time, Pallas kernels for 0%

commit v1 on v0

v1 whole, which is shorter than its diff:
```python
import jax
import jax.numpy as jnp
from jax import lax
from jax.experimental import pallas as pl
from jax.experimental.pallas import tpu as pltpu
from jax.sharding import PartitionSpec as P

DIRECTIONS = ((-1, 0), (1, 0), (0, -1), (0, 1), (-1, -1), (-1, 1), (1, -1), (1, 1))
OPPOSITE = (1, 0, 3, 2, 7, 6, 5, 4)
BF = jnp.bfloat16
F32 = jnp.float32


def leaky(values):
    return jnp.where(values > 0, values, 0.01 * values)


def kernel(
    volume, w1, b1, w2, b2, wi, bi, wo, bo,
    out,
    vbuf, w1b, w2b, wib, wob, b1b, b2b, bib, bob,
    sums, blocks, pads, edge_out, edge_in, corner_out, corner_in,
    load_sem, send_sem, recv_sem,
):
    ix, iy = lax.axis_index("tx"), lax.axis_index("ty")
    nx, ny = lax.axis_size("tx"), lax.axis_size("ty")
    groups_x, groups_y = pads.shape[2] - 2, pads.shape[3] - 2
    half = groups_x * groups_y * 8

    def exists(d):
        dx, dy = DIRECTIONS[d]
        test = None
        for delta, i, n in ((dx, ix, nx), (dy, iy, ny)):
            if delta:
                one = i >= 1 if delta < 0 else i <= n - 2
                test = one if test is None else jnp.logical_and(test, one)
        return test

    def device(d):
        return {"tx": ix + DIRECTIONS[d][0], "ty": iy + DIRECTIONS[d][1]}

    loads = []

    def load(src, dst):
        copy = pltpu.make_async_copy(src, dst, load_sem.at[len(loads)])
        copy.start()
        loads.append(copy)
        return copy

    load_w1, load_b1 = load(w1, w1b), load(b1, b1b)
    load_v = [load(volume.at[pl.ds(8 * i, 8)], vbuf.at[i]) for i in range(groups_x)]
    load_w2, load_b2 = load(w2, w2b), load(b2, b2b)
    load_bi, load_bo = load(bi, bib), load(bo, bob)
    load_wi = {a: load(wi.at[a], wib.at[a]) for a in (1, 0, 2)}
    load_wo = {a: load(wo.at[a], wob.at[a]) for a in (1, 0, 2)}

    barrier = pltpu.get_barrier_semaphore()
    count = 0
    for d in range(8):
        count = count + exists(d).astype(jnp.int32)

        @pl.when(exists(d))
        def _():
            pl.semaphore_signal(
                barrier, inc=1, device_id=device(d), device_id_type=pl.DeviceIdType.MESH
            )

    pads[...] = jnp.zeros_like(pads)

    load_w1.wait()
    load_b1.wait()
    w1cat = jnp.concatenate(
        [
            jnp.concatenate([w1b[p, q, 0], w1b[p, q, 1]], axis=1)
            for p in range(2)
            for q in range(2)
        ],
        axis=0,
    )
    rows_y = 2 * groups_y
    bias1 = b1b[...]
    for i in range(groups_x):
        load_v[i].wait()
        for xp in range(2):
            slabs = [
                vbuf[i, 4 * xp + j].reshape(rows_y, 4, 16, 64) for j in range(4)
            ]
            for pc in range(2):
                for qc in range(2):
                    lhs = jnp.concatenate(
                        [
                            slabs[2 * pc + p][:, 2 * qc + q].reshape(rows_y * 16, 64)
                            for p in range(2)
                            for q in range(2)
                        ],
                        axis=1,
                    )
                    slot = (i * 2 + xp) * 4 + pc * 2 + qc
                    both = jnp.dot(lhs, w1cat, preferred_element_type=F32)
                    sums[slot, 0] = both[:, 0:128]
                    sums[slot, 1] = both[:, 128:256]
            for pc in range(2):
                for qc in range(2):
                    slot = (i * 2 + xp) * 4 + pc * 2 + qc
                    for rc in range(2):
                        even = sums[slot, 0, pl.ds(2 * rc, 4 * rows_y, stride=4)]
                        odd = sums[slot, 1, pl.ds(2 * rc + 1, 4 * rows_y, stride=4)]
                        finer = leaky(even + odd + bias1).astype(BF)
                        k = (pc * 2 + qc) * 2 + rc
                        row = (i * 2 + xp) * 4 * rows_y
                        blocks[row : row + 4 * rows_y, k * 128 : k * 128 + 128] = finer

    load_w2.wait()
    load_b2.wait()
    total = jnp.dot(
        blocks[...], w2b[...].reshape(8 * 128, 256), preferred_element_type=F32
    )
    coarse = leaky(total + b2b[...]).astype(BF).astype(F32)
    coarse = coarse.reshape(groups_x, 2, groups_y * 8, 256)
    even_x = coarse[:, 0].reshape(half, 256)
    odd_x = coarse[:, 1].reshape(half, 256)
    keep = (lax.broadcasted_iota(jnp.int32, (half, 256), 0) // 2) % 2 == 0
    cells = (
        jnp.where(keep, even_x, pltpu.roll(odd_x, 2, 0)),
        jnp.where(keep, pltpu.roll(even_x, half - 2, 0), odd_x),
    )

    def copy_of(e, d, incoming):
        slot = d if incoming else OPPOSITE[d]
        if d < 4:
            src, dst = edge_out.at[e, d], edge_in.at[e, slot]
        else:
            src, dst = corner_out.at[e, d - 4], corner_in.at[e, slot - 4]
        return pltpu.make_async_remote_copy(
            src_ref=src,
            dst_ref=dst,
            send_sem=send_sem.at[e, d],
            recv_sem=recv_sem.at[e, slot],
            device_id=device(d),
            device_id_type=pl.DeviceIdType.MESH,
        )

    def publish(e, cells):
        parts = [c.reshape(groups_x, groups_y, 8, 256) for c in cells]
        for d in (4, 5, 6, 7, 2, 3, 0, 1):
            dx, dy = DIRECTIONS[d]
            sx = slice(0, 1) if dx < 0 else slice(groups_x - 1, groups_x) if dx else slice(None)
            sy = slice(0, 1) if dy < 0 else slice(groups_y - 1, groups_y) if dy else slice(None)
            block = jnp.concatenate(
                [part[sx, sy].reshape(-1, 256) for part in parts], axis=0
            ).astype(BF)
            if d < 4:
                edge_out[e, d] = block
            else:
                corner_out[e, d - 4] = block

            @pl.when(exists(d))
            def _():
                copy_of(e, d, False).start()

        for z in range(2):
            pads[e, z, 1 : 1 + groups_x, 1 : 1 + groups_y] = parts[z]

    def receive(e, d):
        dx, dy = DIRECTIONS[d]
        px = slice(0, 1) if dx < 0 else slice(groups_x + 1, groups_x + 2) if dx else slice(1, 1 + groups_x)
        py = slice(0, 1) if dy < 0 else slice(groups_y + 1, groups_y + 2) if dy else slice(1, 1 + groups_y)

        @pl.when(exists(d))
        def _():
            copy_of(e, d, True).wait_recv()
            block = (edge_in[e, d] if d < 4 else corner_in[e, d - 4]).astype(F32)
            rows = block.shape[0] // 2
            for z in range(2):
                shape = (px.stop - px.start, py.stop - py.start, 8, 256)
                pads[e, z, px, py] = block[z * rows : z * rows + rows].reshape(shape)

    def taps(e, weight, which, totals):
        for a, b in which:
            lhs = jnp.concatenate(
                [
                    pads[e, z, a : a + groups_x, b : b + groups_y].reshape(half, 256).astype(BF)
                    for z in range(2)
                ],
                axis=1,
            )
            lower = weight[a, b, 1:3].reshape(512, 256)
            upper = weight[a, b, 0:2].reshape(512, 256)
            totals = (
                totals[0] + jnp.dot(lhs, lower, preferred_element_type=F32),
                totals[1] + jnp.dot(lhs, upper, preferred_element_type=F32),
            )
        return totals

    def dilated(e, weight, arrivals, start):
        arrivals[1].wait()
        totals = taps(e, weight, ((1, 1),), start)
        for d in (0, 1, 2, 3):
            receive(e, d)
        arrivals[0].wait()
        arrivals[2].wait()
        totals = taps(e, weight, ((0, 1), (2, 1), (1, 0), (1, 2)), totals)
        for d in (4, 5, 6, 7):
            receive(e, d)
        return taps(e, weight, ((0, 0), (0, 2), (2, 0), (2, 2)), totals)

    pl.semaphore_wait(barrier, count)
    publish(0, cells)
    load_bi.wait()
    load_bo.wait()
    inner = jnp.broadcast_to(bib[...], (half, 256))
    totals = dilated(0, wib, load_wi, (inner, inner))
    publish(1, [leaky(t).astype(BF).astype(F32) for t in totals])
    start = [
        pads[0, z, 1 : 1 + groups_x, 1 : 1 + groups_y].reshape(half, 256) + bob[...]
        for z in range(2)
    ]
    totals = dilated(1, wob, load_wo, start)
    lower, upper = leaky(totals[0]), leaky(totals[1])
    even_x = jnp.where(keep, lower, pltpu.roll(upper, 2, 0)).astype(BF)
    odd_x = jnp.where(keep, pltpu.roll(lower, half - 2, 0), upper).astype(BF)
    rows = groups_y * 8
    for i in range(groups_x):
        out[(2 * i) * rows : (2 * i + 1) * rows] = even_x[i * rows : (i + 1) * rows]
        out[(2 * i + 1) * rows : (2 * i + 2) * rows] = odd_x[i * rows : (i + 1) * rows]

    for e in range(2):
        for d in range(8):

            @pl.when(exists(d))
            def _():
                copy_of(e, d, False).wait_send()


def local(
    volume,
    first_weight,
    first_bias,
    second_weight,
    second_bias,
    inner_weight,
    inner_bias,
    outer_weight,
    outer_bias,
):
    size_x, size_y, size_z, chans = volume.shape
    gx, gy = size_x // 8, size_y // 8
    cells = gx * gy * 16
    any_spec = pl.BlockSpec(memory_space=pl.ANY)
    vmem = pltpu.VMEM
    result = pl.pallas_call(
        kernel,
        out_shape=jax.ShapeDtypeStruct((cells, 256), BF),
        in_specs=[any_spec] * 9,
        out_specs=pl.BlockSpec(memory_space=pltpu.VMEM),
        scratch_shapes=[
            vmem((gx, 8, size_y, size_z, chans), BF),
            vmem(first_weight.shape, BF),
            vmem(second_weight.shape, BF),
            vmem(inner_weight.shape, BF),
            vmem(outer_weight.shape, BF),
            vmem((1, 128), F32),
            vmem((1, 256), F32),
            vmem((1, 256), F32),
            vmem((1, 256), F32),
            vmem((gx * 8, 2, gy * 32, 128), F32),
            vmem((cells, 1024), BF),
            vmem((2, 2, gx + 2, gy + 2, 8, 256), F32),
            vmem((2, 4, gy * 16, 256), BF),
            vmem((2, 4, gy * 16, 256), BF),
            vmem((2, 4, 16, 256), BF),
            vmem((2, 4, 16, 256), BF),
            pltpu.SemaphoreType.DMA((gx + 12,)),
            pltpu.SemaphoreType.DMA((2, 8)),
            pltpu.SemaphoreType.DMA((2, 8)),
        ],
        compiler_params=pltpu.CompilerParams(
            collective_id=0, has_side_effects=True, vmem_limit_bytes=56 * 2**20
        ),
        cost_estimate=pl.CostEstimate(
            flops=2_000_000_000, bytes_accessed=12_000_000, transcendentals=0
        ),
    )(
        volume,
        first_weight,
        first_bias.reshape(1, -1),
        second_weight,
        second_bias.reshape(1, -1),
        inner_weight,
        inner_bias.reshape(1, -1),
        outer_weight,
        outer_bias.reshape(1, -1),
    )
    return result.reshape(size_x // 4, size_y // 4, size_z // 4, 256)


def solution(mesh):
    in_specs = (P("tx", "ty", None, None), P(), P(), P(), P(), P(), P(), P(), P())
    out_specs = P("tx", "ty", None, None)
    return jax.shard_map(local, mesh=mesh, in_specs=in_specs, out_specs=out_specs, check_vma=False)
```

time: 123 us -> 17.1 us (0.14)
  the two profiles are of different devices: /device:TPU:11 before, /device:TPU:0 now
where the time goes in v1:
time: 17.1 us; the launch traced here: 17 us
  Pallas kernels  15.4 us (90%)
  local copies, waits for them, and re-layouts  1.6 us (9%)
    pallas_call x1, Pallas kernels, local(): pl.pallas_call(kernel, out_shape=jax.ShapeDtypeStruct((cells, 256), BF),...  15.4 us
    reshape x1, local copies, waits for them, and re-layouts, local(): return result.reshape(size_x // 4, size_y // 4, size_z // 4, 256)  1.6 us

profile of v1, /device:TPU:0, one launch (start us, length us, event | category | flops | bytes accessed | tf_op | source)
XLA Modules:
  0.0 17.0 jit_solution(2417126682819735883)
XLA Ops:
  0.0 15.4 %shard_map.91 = bf16[256,256]{1,0:T(8,128)(2,1)} custom-call(bf16[32,32,16,64]{3,2,1,0:T(8,128)(2,1)} %volume.1, bf16[2,2,2,64,128]{4,3,2,1,0:T(8,128)(2,1)} %w1.1, f32[1,128]{1,0:T(1,128)} %bitcast.7, bf16[2,2,2,128,256]{4,3,2,1,0:T(8,128)(2,1)} %w2.1, f32[1,256]{1,0:T(1,128)} %bitcast.4, bf16[3,3,3,256,256]{4,3,2,1,0:T(8,128)(2,1)} %wi.1, ...), custom_call_target="tpu_custom_call" | custom-call | flops 2000000000 | bytes 12000000 | tf_op jit(solution)/shard_map/pallas_call | solution.py:251
  15.4 1.6 %reshape.19 = bf16[8,8,4,256]{3,2,1,0:T(4,128)(2,1)} reshape(bf16[256,256]{1,0:T(8,128)(2,1)} %shard_map.91) | data formatting | bytes 262144 | tf_op jit(solution)/shard_map/reshape | solution.py:294

commit v2 on v1

--- a/solution.py
+++ b/solution.py
@@ -6,6 +6,7 @@
 from jax.sharding import PartitionSpec as P
 
 DIRECTIONS = ((-1, 0), (1, 0), (0, -1), (0, 1), (-1, -1), (-1, 1), (1, -1), (1, 1))
+ORDER = (4, 5, 6, 7, 2, 3, 0, 1)
 OPPOSITE = (1, 0, 3, 2, 7, 6, 5, 4)
 BF = jnp.bfloat16
 F32 = jnp.float32
@@ -19,12 +20,12 @@
     volume, w1, b1, w2, b2, wi, bi, wo, bo,
     out,
     vbuf, w1b, w2b, wib, wob, b1b, b2b, bib, bob,
-    sums, blocks, pads, edge_out, edge_in, corner_out, corner_in,
+    sums, blocks, halo, inner, edge_out, edge_in, corner_out, corner_in,
     load_sem, send_sem, recv_sem,
 ):
     ix, iy = lax.axis_index("tx"), lax.axis_index("ty")
     nx, ny = lax.axis_size("tx"), lax.axis_size("ty")
-    groups_x, groups_y = pads.shape[2] - 2, pads.shape[3] - 2
+    groups_x, groups_y = halo.shape[1] - 4, halo.shape[2] - 4
     half = groups_x * groups_y * 8
 
     def exists(d):
@@ -65,7 +66,7 @@
                 barrier, inc=1, device_id=device(d), device_id_type=pl.DeviceIdType.MESH
             )
 
-    pads[...] = jnp.zeros_like(pads)
+    halo[...] = jnp.zeros_like(halo)
 
     load_w1.wait()
     load_b1.wait()
@@ -125,97 +126,144 @@
         jnp.where(keep, pltpu.roll(even_x, half - 2, 0), odd_x),
     )
 
-    def copy_of(e, d, incoming):
+    def copy_of(d, incoming):
         slot = d if incoming else OPPOSITE[d]
         if d < 4:
-            src, dst = edge_out.at[e, d], edge_in.at[e, slot]
+            src, dst = edge_out.at[d], edge_in.at[slot]
         else:
-            src, dst = corner_out.at[e, d - 4], corner_in.at[e, slot - 4]
+            src, dst = corner_out.at[d - 4], corner_in.at[slot - 4]
         return pltpu.make_async_remote_copy(
             src_ref=src,
             dst_ref=dst,
-            send_sem=send_sem.at[e, d],
-            recv_sem=recv_sem.at[e, slot],
+            send_sem=send_sem.at[d],
+            recv_sem=recv_sem.at[slot],
             device_id=device(d),
             device_id_type=pl.DeviceIdType.MESH,
         )
 
-    def publish(e, cells):
-        parts = [c.reshape(groups_x, groups_y, 8, 256) for c in cells]
-        for d in (4, 5, 6, 7, 2, 3, 0, 1):
-            dx, dy = DIRECTIONS[d]
-            sx = slice(0, 1) if dx < 0 else slice(groups_x - 1, groups_x) if dx else slice(None)
-            sy = slice(0, 1) if dy < 0 else slice(groups_y - 1, groups_y) if dy else slice(None)
-            block = jnp.concatenate(
-                [part[sx, sy].reshape(-1, 256) for part in parts], axis=0
-            ).astype(BF)
-            if d < 4:
-                edge_out[e, d] = block
-            else:
-                corner_out[e, d - 4] = block
-
-            @pl.when(exists(d))
-            def _():
-                copy_of(e, d, False).start()
-
-        for z in range(2):
-            pads[e, z, 1 : 1 + groups_x, 1 : 1 + groups_y] = parts[z]
-
-    def receive(e, d):
+    def sent(delta, groups):
+        return slice(0, 2) if delta < 0 else slice(groups - 2, groups) if delta else slice(0, groups)
+
+    def landed(delta, groups):
+        if delta < 0:
+            return slice(0, 2)
+        return slice(groups + 2, groups + 4) if delta else slice(2, 2 + groups)
+
+    parts = [c.reshape(groups_x, groups_y, 8, 256) for c in cells]
+    pl.semaphore_wait(barrier, count)
+    for d in ORDER:
         dx, dy = DIRECTIONS[d]
-        px = slice(0, 1) if dx < 0 else slice(groups_x + 1, groups_x + 2) if dx else slice(1, 1 + groups_x)
-        py = slice(0, 1) if dy < 0 else slice(groups_y + 1, groups_y + 2) if dy else slice(1, 1 + groups_y)
+        block = jnp.concatenate(
+            [part[sent(dx, groups_x), sent(dy, groups_y)].reshape(-1, 256) for part in parts],
+            axis=0,
+        ).astype(BF)
+        if d < 4:
+            edge_out[d] = block
+        else:
+            corner_out[d - 4] = block
 
         @pl.when(exists(d))
         def _():
-            copy_of(e, d, True).wait_recv()
-            block = (edge_in[e, d] if d < 4 else corner_in[e, d - 4]).astype(F32)
+            copy_of(d, False).start()
+
+    own = jnp.concatenate([c.astype(BF) for c in cells], axis=1)
+    for z in range(2):
+        halo[z, 2 : 2 + groups_x, 2 : 2 + groups_y] = parts[z]
+    load_bi.wait()
+    load_bo.wait()
+    inner[...] = jnp.broadcast_to(bib[...].reshape(1, 1, 1, 1, 256), inner.shape)
+
+    def both(lhs, weight, a, b):
+        lower = weight[a, b, 1:3].reshape(512, 256)
+        upper = weight[a, b, 0:2].reshape(512, 256)
+        return (
+            jnp.dot(lhs, lower, preferred_element_type=F32),
+            jnp.dot(lhs, upper, preferred_element_type=F32),
+        )
+
+    for a in (1, 0, 2):
+        load_wi[a].wait()
+        for b in (1, 0, 2):
+            for z, term in enumerate(both(own, wib, a, b)):
+                inner[z, 2 - a : 2 - a + groups_x, 2 - b : 2 - b + groups_y] += term.reshape(
+                    groups_x, groups_y, 8, 256
+                )
+
+    for d in ORDER:
+        dx, dy = DIRECTIONS[d]
+        px, py = landed(dx, groups_x), landed(dy, groups_y)
+
+        @pl.when(exists(d))
+        def _():
+            copy_of(d, True).wait_recv()
+            block = (edge_in[d] if d < 4 else corner_in[d - 4]).astype(F32)
             rows = block.shape[0] // 2
             for z in range(2):
                 shape = (px.stop - px.start, py.stop - py.start, 8, 256)
-                pads[e, z, px, py] = block[z * rows : z * rows + rows].reshape(shape)
-
-    def taps(e, weight, which, totals):
-        for a, b in which:
+                halo[z, px, py] = block[z * rows : z * rows + rows].reshape(shape)
+
+    def outside(shift, groups):
+        return [i for i in range(shift, shift + groups + 2) if not 2 <= i < 2 + groups]
+
+    for a in (1, 0, 2):
+        for b in (1, 0, 2):
+            pieces = [
+                (slice(i, i + 1), slice(b, b + groups_y + 2)) for i in outside(a, groups_x)
+            ] + [
+                (slice(2, 2 + groups_x), slice(i, i + 1)) for i in outside(b, groups_y)
+            ]
             lhs = jnp.concatenate(
                 [
-                    pads[e, z, a : a + groups_x, b : b + groups_y].reshape(half, 256).astype(BF)
+                    jnp.concatenate(
+                        [halo[z, sx, sy].reshape(-1, 256) for sx, sy in pieces], axis=0
+                    ).astype(BF)
                     for z in range(2)
                 ],
                 axis=1,
             )
-            lower = weight[a, b, 1:3].reshape(512, 256)
-            upper = weight[a, b, 0:2].reshape(512, 256)
-            totals = (
-                totals[0] + jnp.dot(lhs, lower, preferred_element_type=F32),
-                totals[1] + jnp.dot(lhs, upper, preferred_element_type=F32),
-            )
-        return totals
-
-    def dilated(e, weight, arrivals, start):
-        arrivals[1].wait()
-        totals = taps(e, weight, ((1, 1),), start)
-        for d in (0, 1, 2, 3):
-            receive(e, d)
-        arrivals[0].wait()
-        arrivals[2].wait()
-        totals = taps(e, weight, ((0, 1), (2, 1), (1, 0), (1, 2)), totals)
-        for d in (4, 5, 6, 7):
-            receive(e, d)
-        return taps(e, weight, ((0, 0), (0, 2), (2, 0), (2, 2)), totals)
-
-    pl.semaphore_wait(barrier, count)
-    publish(0, cells)
-    load_bi.wait()
-    load_bo.wait()
-    inner = jnp.broadcast_to(bib[...], (half, 256))
-    totals = dilated(0, wib, load_wi, (inner, inner))
-    publish(1, [leaky(t).astype(BF).astype(F32) for t in totals])
-    start = [
-        pads[0, z, 1 : 1 + groups_x, 1 : 1 + groups_y].reshape(half, 256) + bob[...]
+            for z, term in enumerate(both(lhs, wib, a, b)):
+                row = 0
+                for sx, sy in pieces:
+                    shape = (sx.stop - sx.start, sy.stop - sy.start, 8, 256)
+                    rows = shape[0] * shape[1] * 8
+                    inner[
+                        z, sx.start - a : sx.stop - a, sy.start - b : sy.stop - b
+                    ] += term[row : row + rows].reshape(shape)
+                    row += rows
+
+    inner[...] = leaky(inner[...]).astype(BF).astype(F32)
+
+    @pl.when(ix == 0)
+    def _():
+        inner[:, 0] = jnp.zeros_like(inner[:, 0])
+
+    @pl.when(ix == nx - 1)
+    def _():
+        inner[:, groups_x + 1] = jnp.zeros_like(inner[:, 0])
+
+    @pl.when(iy == 0)
+    def _():
+        inner[:, :, 0] = jnp.zeros_like(inner[:, :, 0])
+
+    @pl.when(iy == ny - 1)
+    def _():
+        inner[:, :, groups_y + 1] = jnp.zeros_like(inner[:, :, 0])
+
+    totals = [
+        halo[z, 2 : 2 + groups_x, 2 : 2 + groups_y].reshape(half, 256) + bob[...]
         for z in range(2)
     ]
-    totals = dilated(1, wob, load_wo, start)
+    for a in (1, 0, 2):
+        load_wo[a].wait()
+        for b in (1, 0, 2):
+            lhs = jnp.concatenate(
+                [
+                    inner[z, a : a + groups_x, b : b + groups_y].reshape(half, 256).astype(BF)
+                    for z in range(2)
+                ],
+                axis=1,
+            )
+            totals = [t + term for t, term in zip(totals, both(lhs, wob, a, b))]
     lower, upper = leaky(totals[0]), leaky(totals[1])
     even_x = jnp.where(keep, lower, pltpu.roll(upper, 2, 0)).astype(BF)
     odd_x = jnp.where(keep, pltpu.roll(lower, half - 2, 0), upper).astype(BF)
@@ -224,12 +272,11 @@
         out[(2 * i) * rows : (2 * i + 1) * rows] = even_x[i * rows : (i + 1) * rows]
         out[(2 * i + 1) * rows : (2 * i + 2) * rows] = odd_x[i * rows : (i + 1) * rows]
 
-    for e in range(2):
-        for d in range(8):
-
-            @pl.when(exists(d))
-            def _():
-                copy_of(e, d, False).wait_send()
+    for d in range(8):
+
+        @pl.when(exists(d))
+        def _():
+            copy_of(d, False).wait_send()
 
 
 def local(
@@ -265,14 +312,15 @@
             vmem((1, 256), F32),
             vmem((gx * 8, 2, gy * 32, 128), F32),
             vmem((cells, 1024), BF),
-            vmem((2, 2, gx + 2, gy + 2, 8, 256), F32),
-            vmem((2, 4, gy * 16, 256), BF),
-            vmem((2, 4, gy * 16, 256), BF),
-            vmem((2, 4, 16, 256), BF),
-            vmem((2, 4, 16, 256), BF),
+            vmem((2, gx + 4, gy + 4, 8, 256), F32),
+            vmem((2, gx + 2, gy + 2, 8, 256), F32),
+            vmem((4, gy * 32, 256), BF),
+            vmem((4, gy * 32, 256), BF),
+            vmem((4, 64, 256), BF),
+            vmem((4, 64, 256), BF),
             pltpu.SemaphoreType.DMA((gx + 12,)),
-            pltpu.SemaphoreType.DMA((2, 8)),
-            pltpu.SemaphoreType.DMA((2, 8)),
+            pltpu.SemaphoreType.DMA((8,)),
+            pltpu.SemaphoreType.DMA((8,)),
         ],
         compiler_params=pltpu.CompilerParams(
             collective_id=0, has_side_effects=True, vmem_limit_bytes=56 * 2**20

time: 17.1 us -> 14.1 us (0.82)
  Pallas kernels: 15.4 us -> 12.4 us
    pallas_call x1, Pallas kernels: 15.4 us -> 12.4 us  [local(): pl.pallas_call(kernel, out_shape=jax.ShapeDtypeStruct((cells, 256), BF),...]
where the time goes in v2:
time: 14.1 us; the launch traced here: 14 us
  Pallas kernels  12.4 us (88%)
  local copies, waits for them, and re-layouts  1.6 us (11%)
    pallas_call x1, Pallas kernels, local(): pl.pallas_call(kernel, out_shape=jax.ShapeDtypeStruct((cells, 256), BF),...  12.4 us
    reshape x1, local copies, waits for them, and re-layouts, local(): return result.reshape(size_x // 4, size_y // 4, size_z // 4, 256)  1.6 us

profile of v2, /device:TPU:0, one launch (start us, length us, event | category | flops | bytes accessed | tf_op | source)
XLA Modules:
  0.0 14.0 jit_solution(11410647466809786443)
XLA Ops:
  0.0 12.4 %shard_map.91 = bf16[256,256]{1,0:T(8,128)(2,1)} custom-call(bf16[32,32,16,64]{3,2,1,0:T(8,128)(2,1)} %volume.1, bf16[2,2,2,64,128]{4,3,2,1,0:T(8,128)(2,1)} %w1.1, f32[1,128]{1,0:T(1,128)} %bitcast.7, bf16[2,2,2,128,256]{4,3,2,1,0:T(8,128)(2,1)} %w2.1, f32[1,256]{1,0:T(1,128)} %bitcast.4, bf16[3,3,3,256,256]{4,3,2,1,0:T(8,128)(2,1)} %wi.1, ...), custom_call_target="tpu_custom_call" | custom-call | flops 2000000000 | bytes 12000000 | tf_op jit(solution)/shard_map/pallas_call | solution.py:298
  12.4 1.6 %reshape.19 = bf16[8,8,4,256]{3,2,1,0:T(4,128)(2,1)} reshape(bf16[256,256]{1,0:T(8,128)(2,1)} %shard_map.91) | data formatting | bytes 262144 | tf_op jit(solution)/shard_map/reshape | solution.py:342

commit v3 on v2

--- a/solution.py
+++ b/solution.py
@@ -5,9 +5,15 @@
 from jax.experimental.pallas import tpu as pltpu
 from jax.sharding import PartitionSpec as P
 
-DIRECTIONS = ((-1, 0), (1, 0), (0, -1), (0, 1), (-1, -1), (-1, 1), (1, -1), (1, 1))
-ORDER = (4, 5, 6, 7, 2, 3, 0, 1)
-OPPOSITE = (1, 0, 3, 2, 7, 6, 5, 4)
+MESSAGES = (
+    (-1, 0, 0), (1, 0, 1),
+    (-1, -1, 0), (-1, 1, 0), (0, -1, 0), (0, 1, 0),
+    (1, -1, 1), (1, 1, 1), (0, -1, 1), (0, 1, 1),
+)
+PARTNER = (1, 0, 7, 6, 5, 4, 3, 2, 9, 8)
+FIRST = (2, 3, 4, 5, 0)
+SECOND = (6, 7, 8, 9, 1)
+NEIGHBOURS = (0, 1, 2, 3, 4, 5, 6, 7)
 BF = jnp.bfloat16
 F32 = jnp.float32
 
@@ -29,7 +35,7 @@
     half = groups_x * groups_y * 8
 
     def exists(d):
-        dx, dy = DIRECTIONS[d]
+        dx, dy, _ = MESSAGES[d]
         test = None
         for delta, i, n in ((dx, ix, nx), (dy, iy, ny)):
             if delta:
@@ -38,7 +44,7 @@
         return test
 
     def device(d):
-        return {"tx": ix + DIRECTIONS[d][0], "ty": iy + DIRECTIONS[d][1]}
+        return {"tx": ix + MESSAGES[d][0], "ty": iy + MESSAGES[d][1]}
 
     loads = []
 
@@ -57,7 +63,7 @@
 
     barrier = pltpu.get_barrier_semaphore()
     count = 0
-    for d in range(8):
+    for d in NEIGHBOURS:
         count = count + exists(d).astype(jnp.int32)
 
         @pl.when(exists(d))
@@ -80,7 +86,7 @@
     )
     rows_y = 2 * groups_y
     bias1 = b1b[...]
-    for i in range(groups_x):
+    def first(i):
         load_v[i].wait()
         for xp in range(2):
             slabs = [
@@ -111,27 +117,12 @@
                         row = (i * 2 + xp) * 4 * rows_y
                         blocks[row : row + 4 * rows_y, k * 128 : k * 128 + 128] = finer
 
-    load_w2.wait()
-    load_b2.wait()
-    total = jnp.dot(
-        blocks[...], w2b[...].reshape(8 * 128, 256), preferred_element_type=F32
-    )
-    coarse = leaky(total + b2b[...]).astype(BF).astype(F32)
-    coarse = coarse.reshape(groups_x, 2, groups_y * 8, 256)
-    even_x = coarse[:, 0].reshape(half, 256)
-    odd_x = coarse[:, 1].reshape(half, 256)
-    keep = (lax.broadcasted_iota(jnp.int32, (half, 256), 0) // 2) % 2 == 0
-    cells = (
-        jnp.where(keep, even_x, pltpu.roll(odd_x, 2, 0)),
-        jnp.where(keep, pltpu.roll(even_x, half - 2, 0), odd_x),
-    )
-
     def copy_of(d, incoming):
-        slot = d if incoming else OPPOSITE[d]
-        if d < 4:
+        slot = d if incoming else PARTNER[d]
+        if d < 2:
             src, dst = edge_out.at[d], edge_in.at[slot]
         else:
-            src, dst = corner_out.at[d - 4], corner_in.at[slot - 4]
+            src, dst = corner_out.at[d - 2], corner_in.at[slot - 2]
         return pltpu.make_async_remote_copy(
             src_ref=src,
             dst_ref=dst,
@@ -141,34 +132,71 @@
             device_id_type=pl.DeviceIdType.MESH,
         )
 
-    def sent(delta, groups):
-        return slice(0, 2) if delta < 0 else slice(groups - 2, groups) if delta else slice(0, groups)
-
-    def landed(delta, groups):
-        if delta < 0:
-            return slice(0, 2)
-        return slice(groups + 2, groups + 4) if delta else slice(2, 2 + groups)
-
-    parts = [c.reshape(groups_x, groups_y, 8, 256) for c in cells]
+    def landed(d):
+        dx, dy, h = MESSAGES[d]
+        if dx:
+            px = slice(0, 2) if dx < 0 else slice(groups_x + 2, groups_x + 4)
+        else:
+            px = slice(2 + 2 * h, 4 + 2 * h)
+        if dy:
+            return px, slice(0, 2) if dy < 0 else slice(groups_y + 2, groups_y + 4)
+        return px, slice(2, 2 + groups_y)
+
+    def second(h):
+        rows = half
+        total = jnp.dot(
+            blocks[h * rows : h * rows + rows],
+            w2b[...].reshape(8 * 128, 256),
+            preferred_element_type=F32,
+        )
+        coarse = leaky(total + b2b[...]).astype(BF).astype(F32)
+        coarse = coarse.reshape(groups_x // 2, 2, groups_y * 8, 256)
+        rows = half // 2
+        even_x = coarse[:, 0].reshape(rows, 256)
+        odd_x = coarse[:, 1].reshape(rows, 256)
+        keep = (lax.broadcasted_iota(jnp.int32, (rows, 256), 0) // 2) % 2 == 0
+        parts = [
+            part.reshape(groups_x // 2, groups_y, 8, 256)
+            for part in (
+                jnp.where(keep, even_x, pltpu.roll(odd_x, 2, 0)),
+                jnp.where(keep, pltpu.roll(even_x, rows - 2, 0), odd_x),
+            )
+        ]
+        for d in SECOND if h else FIRST:
+            dy = MESSAGES[d][1]
+            sy = slice(0, 2) if dy < 0 else slice(groups_y - 2, groups_y) if dy else slice(0, groups_y)
+            block = jnp.concatenate([p[:, sy].reshape(-1, 256) for p in parts], axis=0).astype(BF)
+            if d < 2:
+                edge_out[d] = block
+            else:
+                corner_out[d - 2] = block
+
+            @pl.when(exists(d))
+            def _():
+                copy_of(d, False).start()
+
+        for z in range(2):
+            halo[z, 2 + 2 * h : 4 + 2 * h, 2 : 2 + groups_y] = parts[z]
+
+    per_half = groups_x // 2
+    for i in range(per_half):
+        first(i)
+    load_w2.wait()
+    load_b2.wait()
     pl.semaphore_wait(barrier, count)
-    for d in ORDER:
-        dx, dy = DIRECTIONS[d]
-        block = jnp.concatenate(
-            [part[sent(dx, groups_x), sent(dy, groups_y)].reshape(-1, 256) for part in parts],
-            axis=0,
-        ).astype(BF)
-        if d < 4:
-            edge_out[d] = block
-        else:
-            corner_out[d - 4] = block
-
-        @pl.when(exists(d))
-        def _():
-            copy_of(d, False).start()
-
-    own = jnp.concatenate([c.astype(BF) for c in cells], axis=1)
-    for z in range(2):
-        halo[z, 2 : 2 + groups_x, 2 : 2 + groups_y] = parts[z]
+    second(0)
+    for i in range(per_half, groups_x):
+        first(i)
+    second(1)
+
+    own = jnp.concatenate(
+        [
+            halo[z, 2 : 2 + groups_x, 2 : 2 + groups_y].reshape(half, 256).astype(BF)
+            for z in range(2)
+        ],
+        axis=1,
+    )
+    keep = (lax.broadcasted_iota(jnp.int32, (half, 256), 0) // 2) % 2 == 0
     load_bi.wait()
     load_bo.wait()
     inner[...] = jnp.broadcast_to(bib[...].reshape(1, 1, 1, 1, 256), inner.shape)
@@ -189,14 +217,13 @@
                     groups_x, groups_y, 8, 256
                 )
 
-    for d in ORDER:
-        dx, dy = DIRECTIONS[d]
-        px, py = landed(dx, groups_x), landed(dy, groups_y)
+    for d in FIRST + SECOND:
+        px, py = landed(d)
 
         @pl.when(exists(d))
         def _():
             copy_of(d, True).wait_recv()
-            block = (edge_in[d] if d < 4 else corner_in[d - 4]).astype(F32)
+            block = (edge_in[d] if d < 2 else corner_in[d - 2]).astype(F32)
             rows = block.shape[0] // 2
             for z in range(2):
                 shape = (px.stop - px.start, py.stop - py.start, 8, 256)
@@ -272,7 +299,7 @@
         out[(2 * i) * rows : (2 * i + 1) * rows] = even_x[i * rows : (i + 1) * rows]
         out[(2 * i + 1) * rows : (2 * i + 2) * rows] = odd_x[i * rows : (i + 1) * rows]
 
-    for d in range(8):
+    for d in range(10):
 
         @pl.when(exists(d))
         def _():
@@ -314,13 +341,13 @@
             vmem((cells, 1024), BF),
             vmem((2, gx + 4, gy + 4, 8, 256), F32),
             vmem((2, gx + 2, gy + 2, 8, 256), F32),
-            vmem((4, gy * 32, 256), BF),
-            vmem((4, gy * 32, 256), BF),
-            vmem((4, 64, 256), BF),
-            vmem((4, 64, 256), BF),
+            vmem((2, gy * 32, 256), BF),
+            vmem((2, gy * 32, 256), BF),
+            vmem((8, 64, 256), BF),
+            vmem((8, 64, 256), BF),
             pltpu.SemaphoreType.DMA((gx + 12,)),
-            pltpu.SemaphoreType.DMA((8,)),
-            pltpu.SemaphoreType.DMA((8,)),
+            pltpu.SemaphoreType.DMA((10,)),
+            pltpu.SemaphoreType.DMA((10,)),
         ],
         compiler_params=pltpu.CompilerParams(
             collective_id=0, has_side_effects=True, vmem_limit_bytes=56 * 2**20

time: 14.1 us -> 14 us (level)
  Pallas kernels: 12.4 us -> 12.2 us
    pallas_call x1, Pallas kernels: 12.4 us -> 12.2 us  [local(): pl.pallas_call(kernel, out_shape=jax.ShapeDtypeStruct((cells, 256), BF),...]
where the time goes in v3:
time: 14 us; the launch traced here: 13.8 us
  Pallas kernels  12.2 us (87%)
  local copies, waits for them, and re-layouts  1.6 us (11%)
    pallas_call x1, Pallas kernels, local(): pl.pallas_call(kernel, out_shape=jax.ShapeDtypeStruct((cells, 256), BF),...  12.2 us
    reshape x1, local copies, waits for them, and re-layouts, local(): return result.reshape(size_x // 4, size_y // 4, size_z // 4, 256)  1.6 us

profile of v3, /device:TPU:0, one launch (start us, length us, event | category | flops | bytes accessed | tf_op | source)
XLA Modules:
  0.0 13.8 jit_solution(14368345707265320709)
XLA Ops:
  0.0 12.2 %shard_map.91 = bf16[256,256]{1,0:T(8,128)(2,1)} custom-call(bf16[32,32,16,64]{3,2,1,0:T(8,128)(2,1)} %volume.1, bf16[2,2,2,64,128]{4,3,2,1,0:T(8,128)(2,1)} %w1.1, f32[1,128]{1,0:T(1,128)} %bitcast.7, bf16[2,2,2,128,256]{4,3,2,1,0:T(8,128)(2,1)} %w2.1, f32[1,256]{1,0:T(1,128)} %bitcast.4, bf16[3,3,3,256,256]{4,3,2,1,0:T(8,128)(2,1)} %wi.1, ...), custom_call_target="tpu_custom_call" | custom-call | flops 2000000000 | bytes 12000000 | tf_op jit(solution)/shard_map/pallas_call | solution.py:325
  12.2 1.6 %reshape.19 = bf16[8,8,4,256]{3,2,1,0:T(4,128)(2,1)} reshape(bf16[256,256]{1,0:T(8,128)(2,1)} %shard_map.91) | data formatting | bytes 262144 | tf_op jit(solution)/shard_map/reshape | solution.py:369
